TPU v7x, 256 devices: a whole 4x4x8 slice. The times are simulated.
256 devices in a mesh: dp: 32 (over z_lo, x, core), tp: 8 (over z_hi, y).
Axes of the slice: x: 4, y: 4, z: 8 (z_hi: 2, z_lo: 4; z = z_hi * 4 + z_lo), core: 2. Of those that a mesh axis runs over, the one named last changes fastest.
Arguments:
- tokens: bfloat16 [6144, 3584], P('dp', 'tp'), may hold values from -6 to 6
- cotangent: bfloat16 [6144, 3584], P('dp', 'tp'), may hold values from -6 to 6
- working: bfloat16 [32, 8, 3, 384, 3584], P('dp', 'tp'), may hold values from -0.09375 to 0.09375
- degraded: int32 [32], P('dp'), may hold values from 0 to 1, as said below
- block_map: int32 [32, 16], P('dp'), may hold values from 0 to 7, as said below
- master: float32 [3, 2048, 3584], P(None, ('tp', 'dp')), may hold values from -6 to 6
- moment_one: float32 [3, 2048, 3584], P(None, ('tp', 'dp')), may hold values from -6 to 6
- moment_two: float32 [3, 2048, 3584], P(None, ('tp', 'dp')), may hold values from 0.5 to 8
Outputs:
- input_grad: bfloat16 [6144, 3584], P('dp', 'tp')
- master_next: float32 [3, 2048, 3584], P(None, ('tp', 'dp'))
- moment_one_next: float32 [3, 2048, 3584], P(None, ('tp', 'dp'))
- moment_two_next: float32 [3, 2048, 3584], P(None, ('tp', 'dp'))
Inputs may be any that keep to these rules, and one draw needn't show every extreme that they name: `degraded`: exactly 8 replicas have the value 1. `block_map`: in every row the 16 blocks lie on 6 distinct devices, each of which holds 2 or 3 of them, and at least one holds 3. A row is read only where degraded is 1.
All inputs are finite; a program needn't handle non-finite values.
Results may differ from a plain program's by a relative error of at most 0.0075.
Values may be sent and summed in bfloat16 or wider, within the bound.
A program may use at most 64 MiB of HBM per device.

v0:
```python
import jax
import jax.numpy as jnp
from jax import lax
from jax.sharding import PartitionSpec as P

BLOCK = 128
BLOCKS = 16
beta_one = 0.9
beta_two = 0.95
learn_rate = 0.05
decay_rate = 0.1
adam_eps = 1e-08
bias_one = 1.0 - 0.9**10
bias_two = 1.0 - 0.95**10


def layout_places(replica_flag, mapping, tp_size, slot_count):
    blocks = jnp.arange(BLOCKS, dtype=jnp.int32)
    canonical = blocks // (BLOCKS // tp_size)
    holder = jnp.where(replica_flag > 0, mapping, canonical)
    earlier = (holder[None, :] == holder[:, None]) & (blocks[None, :] < blocks[:, None])
    slot_rank = jnp.sum(earlier.astype(jnp.int32), axis=1)
    return holder * slot_count + slot_rank


def per_device(tokens, cotangent, working, degraded, block_map, master, moment_one, moment_two):
    tp_size = lax.axis_size("tp")
    replicas = lax.axis_size("dp")
    my_index = lax.axis_index("tp")
    weights = working[0, 0]
    slot_count = weights.shape[1] // BLOCK
    per_dev = BLOCKS // tp_size
    places = layout_places(degraded[0], block_map[0], tp_size, slot_count)
    my_slots = my_index * slot_count + jnp.arange(slot_count, dtype=jnp.int32)
    holding = places[:, None] == my_slots[None, :]
    filled = jnp.any(holding, axis=0).astype(jnp.float32)
    column_mask = jnp.repeat(filled, BLOCK)
    inputs, upstream = (
        lax.all_gather(tokens, "tp", axis=1, tiled=True),
        lax.all_gather(cotangent, "tp", axis=1, tiled=True),
    )
    contract_d = (((1,), (1,)), ((), ()))
    gate_pre = lax.dot_general(inputs, weights[0], contract_d, preferred_element_type=jnp.float32)
    up_pre = lax.dot_general(inputs, weights[1], contract_d, preferred_element_type=jnp.float32)
    hidden_grad = lax.dot_general(
        upstream, weights[2], contract_d, preferred_element_type=jnp.float32
    )
    gate_sig = jax.nn.sigmoid(gate_pre)
    active = gate_pre * gate_sig
    hidden = (active * up_pre * column_mask).astype(jnp.bfloat16)
    gate_grad = (
        hidden_grad * up_pre * gate_sig * (1.0 + gate_pre * (1.0 - gate_sig)) * column_mask
    ).astype(jnp.bfloat16)
    up_grad = (hidden_grad * active * column_mask).astype(jnp.bfloat16)
    partial_value = jnp.dot(gate_grad, weights[0], preferred_element_type=jnp.float32) + jnp.dot(
        up_grad, weights[1], preferred_element_type=jnp.float32
    )
    input_grad = lax.psum_scatter(partial_value, "tp", scatter_dimension=1, tiled=True).astype(
        jnp.bfloat16
    )
    tok_rows = gate_grad.shape[0]
    packed = jnp.stack(
        [
            hidden.reshape(tok_rows, slot_count, BLOCK),
            gate_grad.reshape(tok_rows, slot_count, BLOCK),
            up_grad.reshape(tok_rows, slot_count, BLOCK),
        ],
        axis=2,
    )
    packed = packed.transpose(1, 0, 2, 3).reshape(slot_count, tok_rows, 3 * BLOCK)
    wanted = lax.dynamic_slice_in_dim(places, my_index * per_dev, per_dev)
    shard_piece = lax.all_gather(packed, "tp", axis=0, tiled=True)
    positions = jnp.arange(shard_piece.shape[0], dtype=jnp.int32)
    selector = (wanted[:, None] == positions[None, :]).astype(jnp.bfloat16)
    owned_acts = jnp.einsum(
        "kn,ntc->ktc", selector, shard_piece, preferred_element_type=jnp.float32
    ).astype(jnp.bfloat16)
    owned_kinds = (
        owned_acts.reshape(per_dev, tok_rows, 3, BLOCK)
        .transpose(2, 1, 0, 3)
        .reshape(3, tok_rows, per_dev * BLOCK)
    )
    contract_t = (((0,), (0,)), ((), ()))
    gate_term = lax.dot_general(
        owned_kinds[1], inputs, contract_t, preferred_element_type=jnp.float32
    )
    up_term = lax.dot_general(
        owned_kinds[2], inputs, contract_t, preferred_element_type=jnp.float32
    )
    down_term = lax.dot_general(
        owned_kinds[0], upstream, contract_t, preferred_element_type=jnp.float32
    )
    summed = lax.psum_scatter(
        jnp.stack([gate_term, up_term, down_term], axis=1).astype(jnp.bfloat16),
        "dp",
        scatter_dimension=0,
        tiled=True,
    ).astype(jnp.float32)
    grad_mean = jnp.transpose(summed, (1, 0, 2)) / replicas
    moment_one_next = beta_one * moment_one + (1.0 - beta_one) * grad_mean
    moment_two_next = beta_two * moment_two + (1.0 - beta_two) * grad_mean * grad_mean
    update = (
        moment_one_next / bias_one / (jnp.sqrt(moment_two_next / bias_two) + adam_eps)
        + decay_rate * master
    )
    master_next = master - learn_rate * update
    return (input_grad, master_next, moment_one_next, moment_two_next)


def solution(mesh):
    return jax.shard_map(
        per_device,
        mesh=mesh,
        in_specs=(
            P("dp", "tp"),
            P("dp", "tp"),
            P("dp", "tp", None, None, None),
            P("dp"),
            P("dp", None),
            P(None, ("tp", "dp"), None),
            P(None, ("tp", "dp"), None),
            P(None, ("tp", "dp"), None),
        ),
        out_specs=(
            P("dp", "tp"),
            P(None, ("tp", "dp"), None),
            P(None, ("tp", "dp"), None),
            P(None, ("tp", "dp"), None),
        ),
        check_vma=False,
    )
```

profile of v0, /device:TPU:24, one launch (start us, length us, event | category | flops | bytes accessed | tf_op | source)
XLA Modules:
  0.0 538.7 jit_solution(16597101864245584908)
XLA Ops:
  7.2 0.7 all-gather.10.cloned.1.call-update
  7.9 0.7 all-gather.8.cloned.1.call-update
  11.2 71.0 %all-gather.10.cloned.1.call-done = bf16[8,448,192]{1,2,0:T(8,128)(2,1)} async-done(((bf16[1,448,192]{1,2,0:T(8,128)(2,1)}), bf16[8,448,192]{1,2,0:T(8,128)(2,1)}) %all-gather.10.cloned.1.call-update) | async-done | bytes 1376272 | tf_op jit(solution)/shard_map/all_gather | solution.py:39
  82.2 2.3 copy.30
  84.5 1.8 reshape.101
  86.3 63.5 %all-gather.8.cloned.1.call-done = bf16[8,448,192]{1,2,0:T(8,128)(2,1)} async-done(((bf16[1,448,192]{1,2,0:T(8,128)(2,1)}), bf16[8,448,192]{1,2,0:T(8,128)(2,1)}) %all-gather.8.cloned.1.call-update) | async-done | bytes 1376272 | tf_op jit(solution)/shard_map/all_gather | solution.py:40
  149.8 2.3 copy.29
  152.1 2.7 reshape.99
  154.8 2.9 fusion.7
  157.7 2.8 fusion.12
  160.5 3.6 multiply_convert_fusion
  164.8 1.0 stack_reshape.9
  166.8 1.2 reshape.96
  168.0 2.7 fusion.5
  170.7 4.2 convolution_add_fusion
  174.9 4.8 copy.37
  180.1 80.5 %all-gather.6.cloned.1.call-done = bf16[24,192,384]{2,1,0:T(8,128)(2,1)} async-done(((bf16[3,192,384]{2,1,0:T(8,128)(2,1)}), bf16[24,192,384]{2,1,0:T(8,128)(2,1)}) %all-gather.6.cloned.1.call-update) | async-done | bytes 3538960 | tf_op jit(solution)/shard_map/all_gather | solution.py:72
  260.6 4.6 fusion.19
  268.2 0.7 maximum_bitcast_fusion
  269.0 2.8 copy.41
  271.8 107.1 %reduce-scatter.7.cloned.1.call-done = f32[448,192]{1,0:T(8,128)} async-done(((f32[3584,192]{1,0:T(8,128)}), f32[448,192]{1,0:T(8,128)}) %reduce-scatter.7.cloned.1.call-update) | async-done | bytes 344080
  378.9 1.8 copy.38
  380.7 149.4 %reduce-scatter.9.cloned.1.call-done = bf16[8,10752]{1,0:T(8,128)(2,1)} async-done(((bf16[256,10752]{1,0:T(8,128)(2,1)}), bf16[8,10752]{1,0:T(8,128)(2,1)}) %reduce-scatter.9.cloned.1.call-update) | async-done | bytes 172048
  530.1 2.0 multiply_subtract_fusion
  (42 shorter events, 7.0 us)
Async XLA Ops:
  7.2 75.0 %all-gather.10.cloned.1.call-start = ((), (), s32[]{:S(2)}) async-start(), calls=%async_computation.4 | async-start | bytes 1769472 | tf_op jit(solution)/shard_map/all_gather | solution.py:39
  7.9 141.9 %all-gather.8.cloned.1.call-start = ((), (), s32[]{:S(2)}) async-start(), calls=%async_computation.3 | async-start | bytes 1769472 | tf_op jit(solution)/shard_map/all_gather | solution.py:40
  8.6 251.9 %all-gather.6.cloned.1.call-start = ((), (), s32[]{:S(2)}) async-start(), calls=%async_computation.2 | async-start | bytes 3981312 | tf_op jit(solution)/shard_map/all_gather | solution.py:72
  154.8 2.9 copy-start
  164.1 0.7 copy-start.1
  167.9 2.7 copy-start.2
  168.0 210.9 %reduce-scatter.7.cloned.1.call-start = ((), (), s32[]{:S(2)}) async-start(), calls=%async_computation.5 | async-start | bytes 4128768
  179.8 350.3 %reduce-scatter.9.cloned.1.call-start = ((), (), s32[]{:S(2)}) async-start(), calls=%async_computation.6 | async-start | bytes 5677056
  271.8 258.3 %copy-start.3 = (f32[3,8,3584]{2,1,0:T(8,128)S(1)}, f32[3,8,3584]{2,1,0:T(8,128)}, u32[]{:S(2)}) copy-start(f32[3,8,3584]{2,1,0:T(8,128)} %param.13) | copy-start | bytes 1032196
  271.8 258.3 %copy-start.4 = (f32[3,8,3584]{2,1,0:T(8,128)S(1)}, f32[3,8,3584]{2,1,0:T(8,128)}, u32[]{:S(2)}) copy-start(f32[3,8,3584]{2,1,0:T(8,128)} %param.14) | copy-start | bytes 1032196
  271.8 258.3 %copy-start.5 = (f32[3,8,3584]{2,1,0:T(8,128)S(1)}, f32[3,8,3584]{2,1,0:T(8,128)}, u32[]{:S(2)}) copy-start(f32[3,8,3584]{2,1,0:T(8,128)} %param.15) | copy-start | bytes 1032196
Sparse Core Ops, SparseCore 0:
  10.6 71.5 all-gather.9
  84.8 64.9 all-gather.7
  168.1 92.4 all-gather.5
  264.7 114.1 reduce-scatter.6
  381.4 148.5 reduce-scatter.8
where the time goes:
time: 539 us
  waiting for transfers between devices  473 us (88%)
  local copies, waits for them, and re-layouts  22.9 us (4%)
  matrix products  22.8 us (4%)
  between operations  14.6 us (3%)
    unnamed x7, waiting for transfers between devices  258 us
    all_gather x1, waiting for transfers between devices, per_device(): shard_piece = lax.all_gather(packed, 'tp', axis=0, tiled=True)  80.5 us
    all_gather x1, waiting for transfers between devices, per_device(): lax.all_gather(tokens, 'tp', axis=1, tiled=True)  71 us
    all_gather x1, waiting for transfers between devices, per_device(): lax.all_gather(cotangent, 'tp', axis=1, tiled=True)  63.5 us
    unnamed x17, local copies, waits for them, and re-layouts  14.5 us
  transfers between devices with their start and end apart: 5, of which 5 were waited for; matrix products, arithmetic and copies ran while one was open for 6% of the time, Pallas kernels for 0%

commit v1 on v0

--- a/solution.py
+++ b/solution.py
@@ -12,6 +12,12 @@
 adam_eps = 1e-08
 bias_one = 1.0 - 0.9**10
 bias_two = 1.0 - 0.95**10
+carry_the_ratios = lambda pos_dim, field_in: jnp.concatenate(
+    lax.all_to_all(
+        jnp.stack([field_in] * lax.axis_size("tp")), axis_name="tp", split_axis=0, concat_axis=0
+    ),
+    pos_dim,
+)
 
 
 def layout_places(replica_flag, mapping, tp_size, slot_count):
@@ -36,7 +42,7 @@
     filled = jnp.any(holding, axis=0).astype(jnp.float32)
     column_mask = jnp.repeat(filled, BLOCK)
     inputs, upstream = (
-        lax.all_gather(tokens, "tp", axis=1, tiled=True),
+        carry_the_ratios(1, tokens),
         lax.all_gather(cotangent, "tp", axis=1, tiled=True),
     )
     contract_d = (((1,), (1,)), ((), ()))

time: 539 us -> 493 us (0.915)
  waiting for transfers between devices: 473 us -> 416 us
  starting transfers between devices: 0.38 us -> 11.6 us
    all_gather x1 -> x0, waiting for transfers between devices: 71 us -> none  [per_device(): lax.all_gather(tokens, 'tp', axis=1, tiled=True)]
    all_to_all x0 -> x1, waiting for transfers between devices: none -> 27.7 us  [lax.all_to_all(jnp.stack([field_in] * lax.axis_size('tp')), axis_name='tp...]
    all_gather x1, waiting for transfers between devices: 63.5 us -> 51.1 us  [per_device(): lax.all_gather(cotangent, 'tp', axis=1, tiled=True)]
    all_to_all x0 -> x1, starting transfers between devices: none -> 11.3 us  [lax.all_to_all(jnp.stack([field_in] * lax.axis_size('tp')), axis_name='tp...]
    unnamed x17 -> x18, local copies, waits for them, and re-layouts: 14.5 us -> 12.7 us
    unnamed x7 -> x6, waiting for transfers between devices: 258 us -> 257 us
where the time goes in v1:
time: 493 us
  waiting for transfers between devices  416 us (84%)
  local copies, waits for them, and re-layouts  23.7 us (5%)
  matrix products  22.8 us (5%)
  between operations  14.6 us (3%)
  starting transfers between devices  11.6 us (2%)
    unnamed x6, waiting for transfers between devices  257 us
    all_gather x1, waiting for transfers between devices, per_device(): shard_piece = lax.all_gather(packed, 'tp', axis=0, tiled=True)  80.5 us
    all_gather x1, waiting for transfers between devices, per_device(): lax.all_gather(cotangent, 'tp', axis=1, tiled=True)  51.1 us
    all_to_all x1, waiting for transfers between devices, lax.all_to_all(jnp.stack([field_in] * lax.axis_size('tp')), axis_name='tp...  27.7 us
    unnamed x18, local copies, waits for them, and re-layouts  12.7 us
    all_to_all x1, starting transfers between devices, lax.all_to_all(jnp.stack([field_in] * lax.axis_size('tp')), axis_name='tp...  11.3 us
  transfers between devices with their start and end apart: 5, of which 5 were waited for; matrix products, arithmetic and copies ran while one was open for 6% of the time, Pallas kernels for 0%

profile of v1, /device:TPU:24, one launch (start us, length us, event | category | flops | bytes accessed | tf_op | source)
XLA Modules:
  0.0 492.9 jit_solution(7930840731881694501)
XLA Ops:
  7.2 2.2 stack.30
  9.4 11.3 %all-to-all-start = ((bf16[8,192,448]{2,1,0:T(8,128)(2,1)}), bf16[8,192,448]{2,1,0:T(8,128)(2,1)S(1)}, u32[]{:S(2)}, u32[]{:S(2)}) async-start(bf16[8,192,448]{2,1,0:T(8,128)(2,1)} %stack.30), calls=%async_computation | async-start | bytes 3145728 | tf_op jit(solution)/shard_map/all_to_all | solution.py:16
  22.6 27.7 %all-to-all-done = bf16[8,192,448]{2,1,0:T(8,128)(2,1)S(1)} async-done(((bf16[8,192,448]{2,1,0:T(8,128)(2,1)}), bf16[8,192,448]{2,1,0:T(8,128)(2,1)S(1)}, u32[]{:S(2)}, u32[]{:S(2)}) %all-to-all-start) | async-done | bytes 1376288 | tf_op jit(solution)/shard_map/all_to_all | solution.py:16
  50.4 0.9 copy.29
  51.3 1.8 reshape.105
  53.1 51.1 %all-gather.6.cloned.1.call-done = bf16[8,448,192]{1,2,0:T(8,128)(2,1)} async-done(((bf16[1,448,192]{1,2,0:T(8,128)(2,1)}), bf16[8,448,192]{1,2,0:T(8,128)(2,1)}) %all-gather.6.cloned.1.call-update) | async-done | bytes 1376272 | tf_op jit(solution)/shard_map/all_gather | solution.py:46
  104.2 2.3 copy.28
  106.4 2.7 reshape.109
  109.1 2.9 fusion.7
  112.1 2.8 fusion.12
  114.9 3.6 multiply_convert_fusion
  119.2 1.0 stack_reshape.9
  121.1 1.2 reshape.106
  122.4 2.7 fusion.5
  125.0 4.2 convolution_add_fusion
  129.2 4.8 copy.36
  134.4 80.5 %all-gather.4.cloned.1.call-done = bf16[24,192,384]{2,1,0:T(8,128)(2,1)} async-done(((bf16[3,192,384]{2,1,0:T(8,128)(2,1)}), bf16[24,192,384]{2,1,0:T(8,128)(2,1)}) %all-gather.4.cloned.1.call-update) | async-done | bytes 3538960 | tf_op jit(solution)/shard_map/all_gather | solution.py:78
  214.9 4.6 fusion.19
  222.6 0.7 maximum_bitcast_fusion
  223.3 2.8 copy.40
  226.1 106.9 %reduce-scatter.7.cloned.1.call-done = f32[448,192]{1,0:T(8,128)} async-done(((f32[3584,192]{1,0:T(8,128)}), f32[448,192]{1,0:T(8,128)}) %reduce-scatter.7.cloned.1.call-update) | async-done | bytes 344080
  333.1 1.8 copy.37
  334.9 149.4 %reduce-scatter.9.cloned.1.call-done = bf16[8,10752]{1,0:T(8,128)(2,1)} async-done(((bf16[256,10752]{1,0:T(8,128)(2,1)}), bf16[8,10752]{1,0:T(8,128)(2,1)}) %reduce-scatter.9.cloned.1.call-update) | async-done | bytes 172048
  484.3 2.0 multiply_subtract_fusion
  (44 shorter events, 6.3 us)
Async XLA Ops:
  7.2 15.0 %copy-start.6 = (s32[1,16]{1,0:T(1,128)S(1)}, s32[1,16]{1,0:T(1,128)}, u32[]{:S(2)}) copy-start(s32[1,16]{1,0:T(1,128)} %param.12) | copy-start | bytes 196
  9.4 41.0 %all-to-all-start = ((bf16[8,192,448]{2,1,0:T(8,128)(2,1)}), bf16[8,192,448]{2,1,0:T(8,128)(2,1)S(1)}, u32[]{:S(2)}, u32[]{:S(2)}) async-start(bf16[8,192,448]{2,1,0:T(8,128)(2,1)} %stack.30), calls=%async_computation | async-start | bytes 3145728 | tf_op jit(solution)/shard_map/all_to_all | solution.py:16
  20.7 83.5 %all-gather.6.cloned.1.call-start = ((), (), s32[]{:S(2)}) async-start(), calls=%async_computation.4 | async-start | bytes 1769472 | tf_op jit(solution)/shard_map/all_gather | solution.py:46
  21.4 193.5 %all-gather.4.cloned.1.call-start = ((), (), s32[]{:S(2)}) async-start(), calls=%async_computation.3 | async-start | bytes 3981312 | tf_op jit(solution)/shard_map/all_gather | solution.py:78
  109.1 2.9 copy-start
  118.5 0.7 copy-start.1
  122.3 2.7 copy-start.2
  122.3 210.7 %reduce-scatter.7.cloned.1.call-start = ((), (), s32[]{:S(2)}) async-start(), calls=%async_computation.5 | async-start | bytes 4128768
  134.1 350.2 %reduce-scatter.9.cloned.1.call-start = ((), (), s32[]{:S(2)}) async-start(), calls=%async_computation.6 | async-start | bytes 5677056
  226.1 258.2 %copy-start.3 = (f32[3,8,3584]{2,1,0:T(8,128)S(1)}, f32[3,8,3584]{2,1,0:T(8,128)}, u32[]{:S(2)}) copy-start(f32[3,8,3584]{2,1,0:T(8,128)} %param.13) | copy-start | bytes 1032196
  226.1 258.2 %copy-start.4 = (f32[3,8,3584]{2,1,0:T(8,128)S(1)}, f32[3,8,3584]{2,1,0:T(8,128)}, u32[]{:S(2)}) copy-start(f32[3,8,3584]{2,1,0:T(8,128)} %param.14) | copy-start | bytes 1032196
  226.1 258.2 %copy-start.5 = (f32[3,8,3584]{2,1,0:T(8,128)S(1)}, f32[3,8,3584]{2,1,0:T(8,128)}, u32[]{:S(2)}) copy-start(f32[3,8,3584]{2,1,0:T(8,128)} %param.15) | copy-start | bytes 1032196
Sparse Core Ops, SparseCore 0:
  24.1 79.9 all-gather.5
  122.4 92.4 all-gather.3
  219.2 113.7 reduce-scatter.6
  335.6 148.6 reduce-scatter.8
